TPU v7x, 32 devices: a whole 2x2x4 slice. The times are simulated.
32 devices in a mesh: grp: 2 (over x), frame: 16 (over z, y, core).
Axes of the slice: x: 2, y: 2, z: 4, core: 2. Of those that a mesh axis runs over, the one named last changes fastest.
Arguments:
- mixer_input: bfloat16 [8192, 2048], P(('grp', 'frame')), parts along dimension 0, may hold values from -6 to 6
- state_input: bfloat16 [8192, 128], P(('grp', 'frame')), parts along dimension 0, may hold values from -0.08984375 to 0.08984375
- state_output: bfloat16 [8192, 128], P(('grp', 'frame')), parts along dimension 0, may hold values from -0.08984375 to 0.08984375
- log_decay: float32 [8192, 32], P(('grp', 'frame')), parts along dimension 0, may hold values from -1 to 0
- queries: bfloat16 [8192, 2048], P(('grp', 'frame')), parts along dimension 0, may hold values from -6 to 6
- attn_keys: bfloat16 [8192, 2048], P(('grp', 'frame')), parts along dimension 0, may hold values from -6 to 6
- out_grad: bfloat16 [8192, 2048], P(('grp', 'frame')), parts along dimension 0, may hold values from -6 to 6
- frame_offsets: int32 [64], P('grp'), parts along dimension 0, may hold values from 1 to 2, as said below
- sink_frame_index: int32 [2], P('grp'), parts along dimension 0, may hold values from 0 to 31
Outputs:
- grad_input: bfloat16 [8192, 2048], P(('grp', 'frame')), parts along dimension 0
- grad_queries: bfloat16 [8192, 2048], P(('grp', 'frame')), parts along dimension 0
- grad_keys: bfloat16 [8192, 2048], P(('grp', 'frame')), parts along dimension 0
- grad_state_input: float32 [8192, 128], P(('grp', 'frame')), parts along dimension 0
- grad_state_output: float32 [8192, 128], P(('grp', 'frame')), parts along dimension 0
There are 2 independent parts, one for each index of `grp`. A program takes and returns all parts, laid end to end along the dimension named above; each array names one. Nothing has to cross between parts.
Inputs may be any that keep to these rules, and one draw needn't show every extreme that they name: `frame_offsets`: both 1 and 2 occur in every clip.
All inputs are finite; a program needn't handle non-finite values.
Results may differ from a plain program's by a relative error of at most 0.0095.
Values may be sent and summed in bfloat16 or wider, within the bound.
A program may use at most 256 MiB of HBM per device.

v0:
```python
import jax
import jax.numpy as jnp
from jax import lax
from jax.sharding import PartitionSpec as P

DI = 2048
HEADDIM = 64
NSTATE = 128
ATTENTION_WIDTH = 128
S = 128
FR_DEV = 2
OFFMAX = 2
highest = lax.Precision.HIGHEST


def from_behind(value, axis, by):
    peers = lax.axis_size(axis)
    pairs = [(i, i + by) for i in range(peers) if 0 <= i + by < peers]
    return lax.ppermute(value, axis, pairs)


def spread_2(value, axis, root):
    mine = lax.axis_index(axis) == root
    return lax.psum(jnp.where(mine, value, jnp.zeros_like(value)), axis)


def entering(part, axis, combine, identity, reverse):
    count = lax.axis_size(axis)
    place = lax.axis_index(axis)
    ahead = count - 1 - place if reverse else place
    gathered = jax.tree.map(lambda a: lax.all_gather(a, axis), part)
    state = jax.tree.map(lambda a, e: jnp.zeros_like(a) + jnp.asarray(e, a.dtype), part, identity)

    def one(turn, state):
        source = count - 1 - turn if reverse else turn
        return combine(
            state, jax.tree.map(lambda a: lax.dynamic_index_in_dim(a, source, 0, False), gathered)
        )

    return lax.fori_loop(0, ahead, one, state)


def block_local(x_block, b_block, c_block, decay_block, dout_block):
    head_count = DI // HEADDIM
    cumulative = jnp.cumsum(decay_block, axis=0)
    ending = cumulative[-1]
    token_positions = jnp.arange(S)
    lower = (token_positions[:, None] >= token_positions[None, :])[None]
    spread = cumulative.T[:, :, None] - cumulative.T[:, None, :]
    weights = jnp.where(lower, jnp.exp(jnp.where(lower, spread, 0.0)), 0.0)
    inner_cb = jnp.dot(c_block, b_block.T, preferred_element_type=jnp.float32)
    mixing = (weights * inner_cb[None]).astype(jnp.bfloat16)
    x_heads = x_block.reshape(S, head_count, HEADDIM)
    d_heads = dout_block.reshape(S, head_count, HEADDIM)
    dx_inner = jnp.einsum("hts,thp->shp", mixing, d_heads, preferred_element_type=jnp.float32)
    pair_dots = jnp.einsum("thp,shp->hts", d_heads, x_heads, preferred_element_type=jnp.float32)
    folded = jnp.sum(weights * pair_dots, axis=0).astype(jnp.bfloat16)
    grad_b = jnp.dot(folded.T, c_block, preferred_element_type=jnp.float32)
    grad_c = jnp.dot(folded, b_block, preferred_element_type=jnp.float32)
    to_end = jnp.exp(ending[None, :] - cumulative)
    x_scaled = to_end[:, :, None] * x_heads.astype(jnp.float32)
    d_scaled = jnp.exp(cumulative)[:, :, None] * d_heads.astype(jnp.float32)
    state_part = jnp.einsum("shp,sn->hpn", x_scaled, b_block.astype(jnp.float32), precision=highest)
    partial_gradient = jnp.einsum(
        "shp,sn->hpn", d_scaled, c_block.astype(jnp.float32), precision=highest
    )
    return (
        ending,
        to_end,
        x_scaled,
        d_scaled,
        state_part,
        partial_gradient,
        dx_inner,
        grad_b,
        grad_c,
    )


def join_forward(earlier, later):
    return (earlier[0] + later[0], jnp.exp(later[0])[:, None, None] * earlier[1] + later[1])


def join_reverse(earlier, later):
    return (earlier[0] + later[0], later[1] + jnp.exp(later[0])[:, None, None] * earlier[1])


def group_grads(query_g, key_g, value_g, dout_g, score_scale):
    frame_total, row_count, group_width = query_g.shape
    key_rows = key_g.shape[1]
    query_h = query_g.reshape(frame_total, row_count, -1, ATTENTION_WIDTH)
    key_h = key_g.reshape(frame_total, key_rows, -1, ATTENTION_WIDTH)
    value_h = value_g.reshape(frame_total, key_rows, -1, ATTENTION_WIDTH)
    dout_h = dout_g.reshape(frame_total, row_count, -1, ATTENTION_WIDTH)
    scores = (
        jnp.einsum("fqhd,fkhd->fhqk", query_h, key_h, preferred_element_type=jnp.float32)
        * score_scale
    )
    maxima = jnp.max(scores, axis=-1)
    log_norm = maxima + jnp.log(jnp.sum(jnp.exp(scores - maxima[..., None]), axis=-1))
    attn_probs = jnp.exp(scores - log_norm[..., None])
    probs_b = attn_probs.astype(jnp.bfloat16)
    attn_out = jnp.einsum("fhqk,fkhd->fqhd", probs_b, value_h, preferred_element_type=jnp.float32)
    deltas = jnp.sum(dout_h.astype(jnp.float32) * attn_out, axis=-1).transpose(0, 2, 1)
    dprobs = jnp.einsum("fqhd,fkhd->fhqk", dout_h, value_h, preferred_element_type=jnp.float32)
    dscore_b = (attn_probs * (dprobs - deltas[..., None])).astype(jnp.bfloat16)
    grad_q = (
        jnp.einsum("fhqk,fkhd->fqhd", dscore_b, key_h, preferred_element_type=jnp.float32)
        * score_scale
    )
    key_summands = (
        jnp.einsum("fhqk,fqhd->fkhd", dscore_b, query_h, preferred_element_type=jnp.float32)
        * score_scale
    )
    content_summands = jnp.einsum(
        "fhqk,fqhd->fkhd", probs_b, dout_h, preferred_element_type=jnp.float32
    )
    return (
        grad_q.reshape(frame_total, row_count, group_width),
        key_summands.reshape(frame_total, key_rows, group_width),
        content_summands.reshape(frame_total, key_rows, group_width),
        log_norm,
        deltas,
    )


def shards(
    mixer_input,
    state_input,
    state_output,
    log_decay,
    queries,
    attn_keys,
    out_grad,
    frame_offsets,
    sink_frame_index,
):
    row_count = mixer_input.shape[0]
    head_count = DI // HEADDIM
    device = lax.axis_index("frame")
    first_frame = device * FR_DEV
    score_scale = ATTENTION_WIDTH ** (-0.5)
    x_blocks = mixer_input.reshape(FR_DEV, S, DI)
    b_blocks = state_input.reshape(FR_DEV, S, NSTATE)
    c_blocks = state_output.reshape(FR_DEV, S, NSTATE)
    decay_blocks = log_decay.reshape(FR_DEV, S, head_count)
    dout_blocks = out_grad.reshape(FR_DEV, S, DI)
    local_parts = [
        block_local(
            x_blocks[block_index],
            b_blocks[block_index],
            c_blocks[block_index],
            decay_blocks[block_index],
            dout_blocks[block_index],
        )
        for block_index in range(FR_DEV)
    ]
    total_decay = jnp.zeros((head_count,), jnp.float32)
    local_state = jnp.zeros((head_count, HEADDIM, NSTATE), jnp.float32)
    for block_index in range(FR_DEV):
        ending = local_parts[block_index][0]
        local_state = jnp.exp(ending)[:, None, None] * local_state + local_parts[block_index][4]
        total_decay = total_decay + ending
    local_grad = jnp.zeros((head_count, HEADDIM, NSTATE), jnp.float32)
    for block_index in reversed(range(FR_DEV)):
        ending = local_parts[block_index][0]
        local_grad = local_parts[block_index][5] + jnp.exp(ending)[:, None, None] * local_grad
    own_pairs = jnp.stack([attn_keys, mixer_input]).reshape(2, FR_DEV, S, DI)
    tails = jnp.stack([attn_keys, mixer_input])
    before_pairs = from_behind(tails, "frame", 1)
    sink_index = sink_frame_index[0]
    sink_owner = sink_index // FR_DEV
    sink_slot = sink_index % FR_DEV
    picked_sink = lax.dynamic_index_in_dim(own_pairs, sink_slot, axis=1, keepdims=False)
    sink_pairs = spread_2(picked_sink, "frame", sink_owner)
    zero_decay = jnp.zeros_like(total_decay)
    zero_state = jnp.zeros_like(local_state)
    state_in = entering(
        (total_decay, local_state), "frame", join_forward, (zero_decay, zero_state), False
    )[1]
    grad_in = entering(
        (total_decay, local_grad), "frame", join_reverse, (zero_decay, zero_state), True
    )[1]
    key_pool = jnp.concatenate([before_pairs.reshape(2, OFFMAX, S, DI), own_pairs], axis=1)
    frame_ids = first_frame + jnp.arange(FR_DEV, dtype=jnp.int32)
    own_offsets = lax.dynamic_slice_in_dim(frame_offsets, first_frame, FR_DEV)
    target = jnp.maximum(frame_ids - own_offsets, 0) - first_frame + OFFMAX
    other_pairs = jnp.take(key_pool, target, axis=1)
    sink_rows = jnp.broadcast_to(sink_pairs[:, None], (2, FR_DEV, S, DI))
    key_sets = jnp.concatenate([own_pairs[0], other_pairs[0], sink_rows[0]], axis=1)
    value_sets = jnp.concatenate([own_pairs[1], other_pairs[1], sink_rows[1]], axis=1)
    query_frames = queries.reshape(FR_DEV, S, DI)
    group_width = min(DI, 512)
    grad_q_list, key_list, value_list, norm_list, delta_list = ([], [], [], [], [])
    for group_index in range(DI // group_width):
        low_col = group_index * group_width
        high_col = low_col + group_width
        results = group_grads(
            query_frames[:, :, low_col:high_col],
            key_sets[:, :, low_col:high_col],
            value_sets[:, :, low_col:high_col],
            dout_blocks[:, :, low_col:high_col],
            score_scale,
        )
        grad_q_list.append(results[0])
        key_list.append(results[1])
        value_list.append(results[2])
        norm_list.append(results[3])
        delta_list.append(results[4])
    grad_q = jnp.concatenate(grad_q_list, axis=-1)
    pair_grads = jnp.stack(
        [jnp.concatenate(key_list, axis=-1), jnp.concatenate(value_list, axis=-1)]
    )
    pool_hits = (target[:, None] == jnp.arange(OFFMAX + FR_DEV)[None, :]).astype(jnp.float32)
    pool_grads = jnp.einsum(
        "fj,cfsd->cjsd", pool_hits, pair_grads[:, :, S : 2 * S], precision=highest
    )
    own_grad = pair_grads[:, :, :S] + pool_grads[:, OFFMAX:]
    returned = from_behind(pool_grads[:, :OFFMAX], "frame", -1)
    padding = jnp.zeros((2, FR_DEV - OFFMAX, S, DI), jnp.float32)
    own_grad = own_grad + jnp.concatenate([padding, returned], axis=1)
    sink_sum = jnp.sum(pair_grads[:, :, 2 * S :], axis=1)
    sink_total = lax.psum(sink_sum, "frame")
    owner_mask = ((jnp.arange(FR_DEV) == sink_slot) & (device == sink_owner)).astype(jnp.float32)
    own_grad = own_grad + owner_mask[None, :, None, None] * sink_total[:, None]
    ssm_list, grad_b_list, grad_c_list = ([], [], [])
    state_now = state_in
    befores = []
    for block_index in range(FR_DEV):
        befores.append(state_now)
        state_now = (
            jnp.exp(local_parts[block_index][0])[:, None, None] * state_now
            + local_parts[block_index][4]
        )
    afters = [None] * FR_DEV
    grad_now = grad_in
    for block_index in reversed(range(FR_DEV)):
        afters[block_index] = grad_now
        grad_now = (
            local_parts[block_index][5]
            + jnp.exp(local_parts[block_index][0])[:, None, None] * grad_now
        )
    for block_index in range(FR_DEV):
        (
            ending,
            to_end,
            x_scaled,
            d_scaled,
            state_part,
            partial_gradient,
            dx_inner,
            grad_b,
            grad_c,
        ) = local_parts[block_index]
        grad_after = afters[block_index]
        dx_outer = to_end[:, :, None] * jnp.einsum(
            "hpn,sn->shp", grad_after, b_blocks[block_index].astype(jnp.float32), precision=highest
        )
        grad_b = grad_b + jnp.einsum("shp,hpn->sn", x_scaled, grad_after, precision=highest)
        grad_c = grad_c + jnp.einsum(
            "shp,hpn->sn", d_scaled, befores[block_index], precision=highest
        )
        ssm_list.append((dx_inner + dx_outer).reshape(S, DI))
        grad_b_list.append(grad_b)
        grad_c_list.append(grad_c)
    ssm_grad = jnp.stack(ssm_list)
    grad_input = (ssm_grad + own_grad[1]).reshape(row_count, DI).astype(jnp.bfloat16)
    grad_queries = grad_q.reshape(row_count, DI).astype(jnp.bfloat16)
    grad_keys = own_grad[0].reshape(row_count, DI).astype(jnp.bfloat16)
    grad_state_input = jnp.concatenate(grad_b_list, axis=0)
    grad_state_output = jnp.concatenate(grad_c_list, axis=0)
    return (grad_input, grad_queries, grad_keys, grad_state_input, grad_state_output)


def solution(mesh):
    placed = (
        P(("grp", "frame"), None),
        P(("grp", "frame"), None),
        P(("grp", "frame"), None),
        P(("grp", "frame"), None),
        P(("grp", "frame"), None),
        P(("grp", "frame"), None),
        P(("grp", "frame"), None),
        P("grp"),
        P("grp"),
    )
    return jax.shard_map(
        shards,
        mesh=mesh,
        in_specs=placed,
        out_specs=(
            P(("grp", "frame"), None),
            P(("grp", "frame"), None),
            P(("grp", "frame"), None),
            P(("grp", "frame"), None),
            P(("grp", "frame"), None),
        ),
        check_vma=False,
    )
```

profile of v0, /device:TPU:31, one launch (start us, length us, event | category | flops | bytes accessed | tf_op | source)
XLA Modules:
  0.0 628.4 jit_solution(10686105482462887097)
XLA Ops:
  7.9 2.4 fusion.47
  14.6 2.1 fusion.122
  29.9 74.6 %all-reduce.3.cloned.1.call-done = bf16[2,128,2048]{2,1,0:T(8,128)(2,1)} async-done(((bf16[2,128,2048]{2,1,0:T(8,128)(2,1)}), bf16[2,128,2048]{2,1,0:T(8,128)(2,1)}) %all-reduce.3.cloned.1.call-update) | async-done | bytes 1048592 | tf_op jit(solution)/shard_map/psum | solution.py:24
  105.7 3.4 maximum_maximum_fusion
  109.2 4.4 gather_fusion
  115.8 2.1 pad_maximum_fusion.4
  119.7 2.7 copy.248
  147.7 2.6 copy.288
  156.6 3.1 copy.259
  159.7 3.9 copy.296
  167.1 2.2 copy.297
  171.3 3.7 copy.298
  177.0 3.8 copy.299
  183.0 2.1 copy.305
  187.2 3.8 copy.307
  191.0 7.4 %maximum_bitcast_fusion = f32[1,2,384,2048]{3,1,2,0:T(2,128)S(1)} fusion(f32[2,384,512]{2,0,1:T(2,128)} %copy.299, f32[2,384,512]{2,0,1:T(2,128)} %copy.298, f32[2,384,512]{2,0,1:T(2,128)S(1)} %copy-done.27, f32[2,384,512]{2,0,1:T(2,128)S(1)} %copy-done.26), kind=kLoop, calls=%fused_computation.7 | loop fusion | flops 4718592 | bytes 12582912 | tf_op jit(solution)/shard_map/stack | solution.py:211
  198.5 3.7 maximum_bitcast_fusion.1
  202.3 2.7 copy-done.1
  204.9 7.3 %maximum_reduce_fusion = f32[2,128,2048]{2,1,0:T(8,128)} fusion(f32[1,2,384,2048]{3,1,2,0:T(2,128)S(1)} %maximum_bitcast_fusion.1, f32[1,2,384,2048]{3,1,2,0:T(2,128)S(1)} %maximum_bitcast_fusion), kind=kLoop, calls=%fused_computation.10 | loop fusion | flops 1572864 | bytes 14680064 | tf_op jit(solution)/shard_map/reduce_sum | solution.py:222
  224.2 11.2 %fusion.1 = f32[2,4,128,2048]{3,1,2,0:T(4,128)S(1)} fusion(f32[1,2,384,2048]{3,1,2,0:T(2,128)} %copy-done.1, f32[1,2,384,2048]{3,1,2,0:T(2,128)} %copy-done, s32[2]{0:T(128)S(1)} %copy-done.83), kind=kOutput, calls=%fused_computation.9 | convolution fusion | flops 53477384 | bytes 20971528 | tf_op jit(solution)/shard_map/fj,cfsd->cjsd/dot_general | solution.py:215
  235.4 4.6 slice.201
  240.0 5.4 collective-permute-start.1
  245.6 65.6 %all-gather.2 = f32[16,1,32]{2,1,0:T(1,128)} all-gather(f32[1,1,32]{2,1,0:T(1,128)S(1)} %copy-done.82), channel_id=1, replica_groups=mesh['grp'=2,'frame'=16] {'frame'}, dimensions={0}, use_global_device_ids=true | all-gather | bytes 2176 | tf_op jit(solution)/shard_map/all_gather | solution.py:31
  328.8 2.3 fusion.42
  335.8 9.6 %fusion.3 = f32[2,2,128,2048]{3,1,2,0:T(2,128)S(1)} fusion(f32[2,2,128,2048]{3,1,2,0:T(2,128)} %collective-permute-done.1, f32[2,4,128,2048]{3,1,2,0:T(4,128)} %copy-done.2, f32[1,2,384,2048]{3,1,2,0:T(2,128)} %copy-done.1, f32[1,2,384,2048]{3,1,2,0:T(2,128)} %copy-done, f32[2,128,2048]{2,1,0:T(8,128)} %all-reduce.5.cloned.1.call-done, f32[2]{0:T(128)S(1)} %copy-done.84), kind=kLoop, calls=%fused_computation.13 | loop fusion | flops 5242880 | bytes 27262984 | tf_op jit(solution)/shard_map/add | solution.py:225
  346.5 2.5 copy.308
  350.4 94.6 %all-gather.6.cloned.1.call-done = f32[512,64,128]{2,1,0:T(8,128)} async-done(((f32[32,64,128]{2,1,0:T(8,128)}), f32[512,64,128]{2,1,0:T(8,128)}) %all-gather.6.cloned.1.call-update) | async-done | bytes 16777232 | tf_op jit(solution)/shard_map/all_gather | solution.py:31
  449.9 122.4 %all-gather.8.cloned.1.call-done = f32[512,64,128]{2,1,0:T(8,128)} async-done(((f32[32,64,128]{2,1,0:T(8,128)}), f32[512,64,128]{2,1,0:T(8,128)}) %all-gather.8.cloned.1.call-update) | async-done | bytes 16777232 | tf_op jit(solution)/shard_map/all_gather | solution.py:31
  572.4 32.5 %while.27 = (s32[]{:T(128)}, f32[32,64,128]{2,1,0:T(8,128)S(1)}, s32[]{:T(128)}, f32[16,32]{1,0:T(8,128)}, f32[16,32,64,128]{3,2,1,0:T(8,128)}, /*index=5*/s32[]{:T(128)}, s32[]{:T(128)}, s32[]{:T(128)}) while((s32[]{:T(128)}, f32[32,64,128]{2,1,0:T(8,128)S(1)}, s32[]{:T(128)}, f32[16,32]{1,0:T(8,128)}, f32[16,32,64,128]{3,2,1,0:T(8,128)}, ...), condition=%wide.region_22.23_spmd, body=%wide.region_21.22_spmd.sunk | while | flops 524293 | bytes 3146239 | solution.py:40
  604.9 3.5 convolution_bitcast_fusion.8
  613.6 3.1 copy.247
  617.4 2.9 fusion.4
  (332 shorter events, 146.3 us)
Async XLA Ops:
  7.2 97.3 %all-reduce.3.cloned.1.call-start = ((), (), s32[]{:S(2)}) async-start(), calls=%async_computation | async-start | bytes 2097152 | tf_op jit(solution)/shard_map/psum | solution.py:24
  10.4 325.4 %all-reduce.5.cloned.1.call-start = ((), (), s32[]{:S(2)}) async-start(), calls=%async_computation.1 | async-start | bytes 4194304 | tf_op jit(solution)/shard_map/psum | solution.py:223
  12.0 93.7 %collective-permute-start = (bf16[2,256,2048]{2,1,0:T(8,128)(2,1)}, bf16[2,256,2048]{2,1,0:T(8,128)(2,1)}, u32[]{:S(2)}, u32[]{:S(2)}) collective-permute-start(bf16[2,256,2048]{2,1,0:T(8,128)(2,1)} %pad_maximum_fusion.7), channel_id=1, source_target_pairs={{0,1},{1,2},{2,3},{3,4},{4,5},{5,6},{6,7},{7,8},{8,9},{9,10},{10,1... | collective-permute-start | bytes 6291464 | tf_op jit(solution)/shard_map/ppermute | solution.py:19
  14.0 200.3 %copy-start.61 = (f32[128,32]{1,0:T(8,128)}, f32[128,32]{1,0:T(8,128)S(1)}, u32[]{:S(2)}) copy-start(f32[128,32]{1,0:T(8,128)S(1)} %reduce_window_sum.18) | copy-start | bytes 49156
  17.7 6.1 copy-start.59
  17.7 7.0 %copy-start.56 = (bf16[2,128,512]{2,1,0:T(8,128)(2,1)S(1)}, bf16[2,128,512]{2,1,0:T(8,128)(2,1)}, u32[]{:S(2)}) copy-start(bf16[2,128,512]{2,1,0:T(8,128)(2,1)} %get-tuple-element.177) | copy-start | bytes 786436
  17.7 7.8 %copy-start.57 = (bf16[2,128,512]{2,1,0:T(8,128)(2,1)S(1)}, bf16[2,128,512]{2,1,0:T(8,128)(2,1)}, u32[]{:S(2)}) copy-start(bf16[2,128,512]{2,1,0:T(8,128)(2,1)} %get-tuple-element.181) | copy-start | bytes 786436
  17.7 9.5 %copy-start.55 = (bf16[2,128,512]{2,1,0:T(8,128)(2,1)S(1)}, bf16[2,128,512]{2,1,0:T(8,128)(2,1)}, u32[]{:S(2)}) copy-start(bf16[2,128,512]{2,1,0:T(8,128)(2,1)} %get-tuple-element.180) | copy-start | bytes 786436
  27.4 186.9 %copy-start.71 = (f32[128,32]{0,1:T(8,128)}, f32[128,32]{0,1:T(8,128)S(1)}, u32[]{:S(2)}) copy-start(f32[128,32]{0,1:T(8,128)S(1)} %copy.241) | copy-start | bytes 49156
  130.1 24.5 %copy-start.17 = (bf16[2,4,128,384]{2,3,1,0:T(8,128)(2,1)}, bf16[2,4,128,384]{2,3,1,0:T(8,128)(2,1)S(1)}, u32[]{:S(2)}) copy-start(bf16[2,4,128,384]{2,3,1,0:T(8,128)(2,1)S(1)} %fusion.17) | copy-start | bytes 2359300
  136.6 27.0 %copy-start.19 = (bf16[2,4,128,384]{2,3,1,0:T(8,128)(2,1)}, bf16[2,4,128,384]{2,3,1,0:T(8,128)(2,1)S(1)}, u32[]{:S(2)}) copy-start(bf16[2,4,128,384]{2,3,1,0:T(8,128)(2,1)S(1)} %fusion.13) | copy-start | bytes 2359300
  145.9 23.3 %copy-start.21 = (bf16[2,4,128,384]{2,3,1,0:T(8,128)(2,1)}, bf16[2,4,128,384]{2,3,1,0:T(8,128)(2,1)S(1)}, u32[]{:S(2)}) copy-start(bf16[2,4,128,384]{2,3,1,0:T(8,128)(2,1)S(1)} %fusion.9) | copy-start | bytes 2359300
  155.0 20.0 %copy-start.22 = (bf16[2,4,128,384]{2,3,1,0:T(8,128)(2,1)}, bf16[2,4,128,384]{2,3,1,0:T(8,128)(2,1)S(1)}, u32[]{:S(2)}) copy-start(bf16[2,4,128,384]{2,3,1,0:T(8,128)(2,1)S(1)} %fusion.5) | copy-start | bytes 2359300
  191.0 7.5 %copy-start.28 = (f32[2,384,512]{2,0,1:T(2,128)S(1)}, f32[2,384,512]{2,0,1:T(2,128)}, u32[]{:S(2)}) copy-start(f32[2,384,512]{2,0,1:T(2,128)} %copy.304) | copy-start | bytes 4718596
  191.0 7.5 %copy-start.29 = (f32[2,384,512]{2,0,1:T(2,128)S(1)}, f32[2,384,512]{2,0,1:T(2,128)}, u32[]{:S(2)}) copy-start(f32[2,384,512]{2,0,1:T(2,128)} %copy.305) | copy-start | bytes 4718596
  191.0 7.5 %copy-start.30 = (f32[2,384,512]{2,0,1:T(2,128)S(1)}, f32[2,384,512]{2,0,1:T(2,128)}, u32[]{:S(2)}) copy-start(f32[2,384,512]{2,0,1:T(2,128)} %copy.306) | copy-start | bytes 4718596
  191.0 7.5 %copy-start.31 = (f32[2,384,512]{2,0,1:T(2,128)S(1)}, f32[2,384,512]{2,0,1:T(2,128)}, u32[]{:S(2)}) copy-start(f32[2,384,512]{2,0,1:T(2,128)} %copy.307) | copy-start | bytes 4718596
  212.3 232.6 %all-gather.6.cloned.1.call-start = ((), (), s32[]{:S(2)}) async-start(), calls=%async_computation.2 | async-start | bytes 17825792 | tf_op jit(solution)/shard_map/all_gather | solution.py:31
  213.9 103.5 %copy-start.39 = (bf16[128,2048]{0,1:T(8,128)(2,1)}, bf16[128,2048]{0,1:T(8,128)(2,1)S(1)}, u32[]{:S(2)}) copy-start(bf16[128,2048]{0,1:T(8,128)(2,1)S(1)} %copy.242) | copy-start | bytes 1572868
  214.3 101.2 %copy-start.35 = (bf16[128,2048]{0,1:T(8,128)(2,1)}, bf16[128,2048]{0,1:T(8,128)(2,1)S(1)}, u32[]{:S(2)}) copy-start(bf16[128,2048]{0,1:T(8,128)(2,1)S(1)} %copy.238) | copy-start | bytes 1572868
  214.3 7.3 %copy-start.78 = (f32[32]{0:T(128)}, f32[32]{0:T(128)S(1)}, u32[]{:S(2)}) copy-start(f32[32]{0:T(128)S(1)} %get-tuple-element.209) | copy-start | bytes 388
  216.7 355.6 %all-gather.8.cloned.1.call-start = ((), (), s32[]{:S(2)}) async-start(), calls=%async_computation.3 | async-start | bytes 17825792 | tf_op jit(solution)/shard_map/all_gather | solution.py:31
  219.3 92.7 %copy-start.40 = (bf16[128,2048]{0,1:T(8,128)(2,1)}, bf16[128,2048]{0,1:T(8,128)(2,1)S(1)}, u32[]{:S(2)}) copy-start(bf16[128,2048]{0,1:T(8,128)(2,1)S(1)} %copy.318) | copy-start | bytes 1572868
  220.9 92.9 %copy-start.37 = (bf16[128,2048]{0,1:T(8,128)(2,1)}, bf16[128,2048]{0,1:T(8,128)(2,1)S(1)}, u32[]{:S(2)}) copy-start(bf16[128,2048]{0,1:T(8,128)(2,1)S(1)} %copy.319) | copy-start | bytes 1572868
  235.4 10.1 %copy-start.62 = (f32[128,32]{1,0:T(8,128)S(1)}, f32[128,32]{1,0:T(8,128)}, u32[]{:S(2)}) copy-start(f32[128,32]{1,0:T(8,128)} %copy-done.61) | copy-start | bytes 49156
  235.4 10.1 %copy-start.82 = (f32[1,1,32]{2,1,0:T(1,128)S(1)}, f32[1,1,32]{2,1,0:T(1,128)}, u32[]{:S(2)}) copy-start(f32[1,1,32]{2,1,0:T(1,128)} %get-tuple-element.190) | copy-start | bytes 388
  240.0 95.7 %collective-permute-start.1 = (f32[2,2,128,2048]{3,1,2,0:T(2,128)}, f32[2,2,128,2048]{3,1,2,0:T(2,128)}, u32[]{:S(2)}, u32[]{:S(2)}) collective-permute-start(f32[2,2,128,2048]{3,1,2,0:T(2,128)} %slice.201), channel_id=1, source_target_pairs={{1,0},{2,1},{3,2},{4,3},{5,4},{6,5},{7,6},{8,7},{9,8},{10,9},{11,1... | collective-permute-start | bytes 12582920 | tf_op jit(solution)/shard_map/ppermute | solution.py:19
  320.4 8.4 %copy-start.14 = (bf16[2,384,512]{1,2,0:T(8,128)(2,1)S(1)}, bf16[2,384,512]{1,2,0:T(8,128)(2,1)}, u32[]{:S(2)}) copy-start(bf16[2,384,512]{1,2,0:T(8,128)(2,1)} %copy-done.13) | copy-start | bytes 2359300
  325.1 7.9 %copy-start.16 = (bf16[2,384,512]{1,2,0:T(8,128)(2,1)S(1)}, bf16[2,384,512]{1,2,0:T(8,128)(2,1)}, u32[]{:S(2)}) copy-start(bf16[2,384,512]{1,2,0:T(8,128)(2,1)} %copy-done.15) | copy-start | bytes 2359300
  325.1 7.9 %copy-start.23 = (bf16[2,4,128,384]{2,3,1,0:T(8,128)(2,1)S(1)}, bf16[2,4,128,384]{2,3,1,0:T(8,128)(2,1)}, u32[]{:S(2)}) copy-start(bf16[2,4,128,384]{2,3,1,0:T(8,128)(2,1)} %copy-done.22) | copy-start | bytes 2359300
  572.4 32.5 %copy-start.72 = (f32[128,32]{0,1:T(8,128)S(1)}, f32[128,32]{0,1:T(8,128)}, u32[]{:S(2)}) copy-start(f32[128,32]{0,1:T(8,128)} %copy-done.71) | copy-start | bytes 49156
  572.4 32.5 %copy-start.81 = (f32[32]{0:T(128)S(1)}, f32[32]{0:T(128)}, u32[]{:S(2)}) copy-start(f32[32]{0:T(128)} %copy-done.80) | copy-start | bytes 388
  (59 other events, 164.3 us)
Sparse Core Ops, SparseCore 0:
  12.0 92.3 all-reduce.2
  212.4 103.4 all-reduce.4
  318.3 126.6 all-gather.5
  447.2 125.0 all-gather.7
where the time goes:
time: 634 us; the launch traced here: 628 us
  waiting for transfers between devices  292 us (46%)
  local copies, waits for them, and re-layouts  112 us (18%)
  other arithmetic  74.6 us (12%)
  blocking collectives  65.6 us (10%)
  matrix products  60.6 us (10%)
  between operations  15.9 us (3%)
  starting transfers between devices  7.4 us (1%)
    all_gather x2, waiting for transfers between devices, entering(): gathered = jax.tree.map(lambda a: lax.all_gather(a, axis), part)  217 us
    psum x1, waiting for transfers between devices, spread_2(): return lax.psum(jnp.where(mine, value, jnp.zeros_like(value)), axis)  74.6 us
    all_gather x1, blocking collectives, entering(): gathered = jax.tree.map(lambda a: lax.all_gather(a, axis), part)  65.6 us
    add x15, other arithmetic, join_forward(): jnp.exp(later[0])[:, None, None] * earlier[1] + later[1]  21.7 us
    reshape x4, local copies, waits for them, and re-layouts, group_grads(): key_summands.reshape(frame_total, key_rows, group_width)  13.6 us
  transfers between devices with their start and end apart: 6, of which 3 were waited for; matrix products, arithmetic and copies ran while one was open for 14% of the time, Pallas kernels for 0%

commit v1 on v0

--- a/solution.py
+++ b/solution.py
@@ -21,7 +21,7 @@
 
 def spread_2(value, axis, root):
     mine = lax.axis_index(axis) == root
-    return lax.psum(jnp.where(mine, value, jnp.zeros_like(value)), axis)
+    return jnp.sum(lax.all_gather(jnp.where(mine, value, jnp.zeros_like(value)), axis), axis=0)
 
 
 def entering(part, axis, combine, identity, reverse):

time: 634 us -> 566 us (0.89)
  the two profiles are of different devices: /device:TPU:31 before, /device:TPU:0 now
where the time goes in v1:
time: 566 us; the launch traced here: 557 us
  waiting for transfers between devices  222 us (39%)
  local copies, waits for them, and re-layouts  117 us (21%)
  other arithmetic  78.3 us (14%)
  matrix products  61.6 us (11%)
  blocking collectives  56.3 us (10%)
  between operations  15.9 us (3%)
  starting transfers between devices  5.71 us (1%)
    all_gather x2, waiting for transfers between devices, entering(): gathered = jax.tree.map(lambda a: lax.all_gather(a, axis), part)  112 us
    psum x1, waiting for transfers between devices, shards(): sink_total = lax.psum(sink_sum, 'frame')  77.1 us
    all_gather x1, blocking collectives, entering(): gathered = jax.tree.map(lambda a: lax.all_gather(a, axis), part)  56.3 us
    all_gather x1, waiting for transfers between devices, spread_2(): lax.all_gather(jnp.where(mine, value, jnp.zeros_like(value)), axis)  32.8 us
    add x15, other arithmetic, join_reverse(): later[1] + jnp.exp(later[0])[:, None, None] * earlier[1]  21.8 us
    reshape x4, local copies, waits for them, and re-layouts, group_grads(): key_summands.reshape(frame_total, key_rows, group_width)  14.9 us
    reshape x4, local copies, waits for them, and re-layouts, group_grads(): content_summands.reshape(frame_total, key_rows, group_width)  13.4 us
    unnamed x188, local copies, waits for them, and re-layouts  12 us
  transfers between devices with their start and end apart: 6, of which 3 were waited for; matrix products, arithmetic and copies ran while one was open for 41% of the time, Pallas kernels for 0%

profile of v1, /device:TPU:0, one launch (start us, length us, event | category | flops | bytes accessed | tf_op | source)
XLA Modules:
  0.0 557.5 jit_solution(6535836097293850537)
XLA Ops:
  7.9 2.4 fusion.46
  22.3 3.8 collective-permute-start
  42.9 56.3 %all-gather.3 = f32[16,1,32]{2,1,0:T(1,128)} all-gather(f32[1,1,32]{2,1,0:T(1,128)} %get-tuple-element.190), channel_id=1, replica_groups=mesh['grp'=2,'frame'=16] {'frame'}, dimensions={0}, use_global_device_ids=true | all-gather | bytes 2176 | tf_op jit(solution)/shard_map/all_gather | solution.py:31
  103.5 2.1 multiply_reduce_fusion.1
  111.3 3.5 maximum_maximum_fusion
  114.9 4.3 gather_fusion
  122.2 32.8 %all-gather.10.cloned.1.call-done = bf16[32,1,128,2048]{3,2,1,0:T(8,128)(2,1)} async-done(((bf16[2,1,128,2048]{3,2,1,0:T(8,128)(2,1)}), bf16[32,1,128,2048]{3,2,1,0:T(8,128)(2,1)}) %all-gather.10.cloned.1.call-update) | async-done | bytes 16777232 | tf_op jit(solution)/shard_map/all_gather | solution.py:24
  155.0 7.2 %bitcast_reduce_fusion = bf16[2,128,2048]{2,1,0:T(8,128)(2,1)S(1)} fusion(bf16[16,2,128,2048]{3,2,1,0:T(8,128)(2,1)} %bitcast.371), kind=kLoop, calls=%fused_computation.5 | loop fusion | flops 7864320 | bytes 17825792 | tf_op jit(solution)/shard_map/reduce_sum | solution.py:24
  167.4 2.6 copy.248
  176.9 2.4 copy.276
  187.2 3.7 copy.296
  196.3 3.0 copy.271
  199.3 3.9 copy.297
  209.1 3.1 copy.283
  212.1 3.7 copy.298
  221.8 3.0 copy.295
  224.8 3.7 copy.299
  228.5 2.6 fusion.79
  231.1 3.7 copy.304
  236.5 3.8 copy.305
  244.5 3.8 copy.307
  248.3 7.4 %maximum_bitcast_fusion = f32[1,2,384,2048]{3,1,2,0:T(2,128)S(1)} fusion(f32[2,384,512]{2,0,1:T(2,128)} %copy.299, f32[2,384,512]{2,0,1:T(2,128)} %copy.298, f32[2,384,512]{2,0,1:T(2,128)S(1)} %copy-done.31, f32[2,384,512]{2,0,1:T(2,128)S(1)} %copy-done.30), kind=kLoop, calls=%fused_computation.8 | loop fusion | flops 4718592 | bytes 12582912 | tf_op jit(solution)/shard_map/stack | solution.py:211
  255.8 3.7 maximum_bitcast_fusion.1
  259.6 11.9 %fusion.1 = f32[2,4,128,2048]{3,1,2,0:T(4,128)} fusion(f32[1,2,384,2048]{3,1,2,0:T(2,128)S(1)} %maximum_bitcast_fusion.1, f32[1,2,384,2048]{3,1,2,0:T(2,128)S(1)} %maximum_bitcast_fusion, s32[2]{0:T(128)S(1)} %copy-done.89), kind=kOutput, calls=%fused_computation.10 | convolution fusion | flops 53477384 | bytes 20971528 | tf_op jit(solution)/shard_map/fj,cfsd->cjsd/dot_general | solution.py:215
  271.5 7.5 %slice.201 = f32[2,2,128,2048]{3,1,2,0:T(2,128)} slice(f32[2,4,128,2048]{3,1,2,0:T(4,128)} %fusion.1), slice={[0:2], [0:2], [0:128], [0:2048]} | slice | bytes 8388608 | tf_op jit(solution)/shard_map/slice | solution.py:219
  280.7 7.3 %maximum_reduce_fusion = f32[2,128,2048]{2,1,0:T(8,128)} fusion(f32[1,2,384,2048]{3,1,2,0:T(2,128)S(1)} %maximum_bitcast_fusion.1, f32[1,2,384,2048]{3,1,2,0:T(2,128)S(1)} %maximum_bitcast_fusion), kind=kLoop, calls=%fused_computation.11 | loop fusion | flops 1572864 | bytes 14680064 | tf_op jit(solution)/shard_map/reduce_sum | solution.py:222
  288.2 32.6 %while.26 = (s32[]{:T(128)}, f32[32,64,128]{2,1,0:T(8,128)S(1)}, s32[]{:T(128)}, f32[16,32,64,128]{3,2,1,0:T(8,128)}, f32[16,32]{1,0:T(8,128)}, /*index=5*/s32[]{:T(128)}, s32[]{:T(128)}, s32[]{:T(128)}, s32[]{:T(128)}) while((s32[]{:T(128)}, f32[32,64,128]{2,1,0:T(8,128)S(1)}, s32[]{:T(128)}, f32[16,32,64,128]{3,2,1,0:T(8,128)}, ...), condition=%wide.region_3.4_spmd, body=%wide.region_2.3_spmd.sunk | while | flops 524294 | bytes 3146259 | solution.py:40
  320.8 112.4 %all-gather.12.cloned.1.call-done = f32[512,64,128]{2,1,0:T(8,128)} async-done(((f32[32,64,128]{2,1,0:T(8,128)}), f32[512,64,128]{2,1,0:T(8,128)}) %all-gather.12.cloned.1.call-update) | async-done | bytes 16777232 | tf_op jit(solution)/shard_map/all_gather | solution.py:31
  436.3 2.5 convolution_bitcast_fusion.9
  451.1 3.3 copy.247
  458.5 77.1 %all-reduce.2.cloned.1.call-done = f32[2,128,2048]{2,1,0:T(8,128)} async-done(((f32[2,128,2048]{2,1,0:T(8,128)}), f32[2,128,2048]{2,1,0:T(8,128)}) %all-reduce.2.cloned.1.call-update) | async-done | bytes 2097168 | tf_op jit(solution)/shard_map/psum | solution.py:223
  535.6 9.5 %fusion.3 = f32[2,2,128,2048]{3,1,2,0:T(2,128)S(1)} fusion(f32[2,2,128,2048]{3,1,2,0:T(2,128)} %collective-permute-done.1, f32[2,4,128,2048]{3,1,2,0:T(4,128)} %fusion.1, f32[1,2,384,2048]{3,1,2,0:T(2,128)} %copy-done.1, f32[1,2,384,2048]{3,1,2,0:T(2,128)} %copy-done, f32[2,128,2048]{2,1,0:T(8,128)} %all-reduce.2.cloned.1.call-done, f32[2]{0:T(128)S(1)} %copy-done.90), kind=kLoop, calls=%fused_computation.14 | loop fusion | flops 5242880 | bytes 27262984 | tf_op jit(solution)/shard_map/add | solution.py:225
  (347 shorter events, 143.0 us)
Async XLA Ops:
  7.2 147.8 %all-gather.10.cloned.1.call-start = ((), (), s32[]{:S(2)}) async-start(), calls=%async_computation.2 | async-start | bytes 17825792 | tf_op jit(solution)/shard_map/all_gather | solution.py:24
  10.3 277.8 %all-gather.8.cloned.1.call-start = ((), (), s32[]{:S(2)}) async-start(), calls=%async_computation.1 | async-start | bytes 17825792 | tf_op jit(solution)/shard_map/all_gather | solution.py:31
  12.0 4.0 copy-start.79
  12.4 95.2 %copy-start.36 = (bf16[128,2048]{0,1:T(8,128)(2,1)}, bf16[128,2048]{0,1:T(8,128)(2,1)S(1)}, u32[]{:S(2)}) copy-start(bf16[128,2048]{0,1:T(8,128)(2,1)S(1)} %copy.238) | copy-start | bytes 1572868
  12.4 5.7 %copy-start.85 = (f32[32]{0:T(128)}, f32[32]{0:T(128)S(1)}, u32[]{:S(2)}) copy-start(f32[32]{0:T(128)S(1)} %get-tuple-element.209) | copy-start | bytes 388
  16.1 417.2 %all-gather.12.cloned.1.call-start = ((), (), s32[]{:S(2)}) async-start(), calls=%async_computation.3 | async-start | bytes 17825792 | tf_op jit(solution)/shard_map/all_gather | solution.py:31
  17.0 88.7 %copy-start.38 = (bf16[128,2048]{0,1:T(8,128)(2,1)}, bf16[128,2048]{0,1:T(8,128)(2,1)S(1)}, u32[]{:S(2)}) copy-start(bf16[128,2048]{0,1:T(8,128)(2,1)S(1)} %copy.319) | copy-start | bytes 1572868
  20.8 514.9 %all-reduce.2.cloned.1.call-start = ((), (), s32[]{:S(2)}) async-start(), calls=%async_computation | async-start | bytes 4194304 | tf_op jit(solution)/shard_map/psum | solution.py:223
  20.8 5.3 copy-start.68
  22.3 4.7 copy-start.46
  22.3 89.0 %collective-permute-start = (bf16[2,256,2048]{2,1,0:T(8,128)(2,1)}, bf16[2,256,2048]{2,1,0:T(8,128)(2,1)}, u32[]{:S(2)}, u32[]{:S(2)}) collective-permute-start(bf16[2,256,2048]{2,1,0:T(8,128)(2,1)} %pad_maximum_fusion.7), channel_id=1, source_target_pairs={{0,1},{1,2},{2,3},{3,4},{4,5},{5,6},{6,7},{7,8},{8,9},{9,10},{10,1... | collective-permute-start | bytes 6291464 | tf_op jit(solution)/shard_map/ppermute | solution.py:19
  114.9 4.3 copy-start.91
  165.6 4.4 copy-start.10
  171.8 4.0 copy-start.54
  174.6 4.7 copy-start.53
  176.9 4.7 copy-start.14
  244.5 3.9 copy-start.31
  248.3 7.5 %copy-start.32 = (f32[2,384,512]{2,0,1:T(2,128)S(1)}, f32[2,384,512]{2,0,1:T(2,128)}, u32[]{:S(2)}) copy-start(f32[2,384,512]{2,0,1:T(2,128)} %copy.304) | copy-start | bytes 4718596
  248.3 7.5 %copy-start.33 = (f32[2,384,512]{2,0,1:T(2,128)S(1)}, f32[2,384,512]{2,0,1:T(2,128)}, u32[]{:S(2)}) copy-start(f32[2,384,512]{2,0,1:T(2,128)} %copy.305) | copy-start | bytes 4718596
  248.3 7.5 %copy-start.34 = (f32[2,384,512]{2,0,1:T(2,128)S(1)}, f32[2,384,512]{2,0,1:T(2,128)}, u32[]{:S(2)}) copy-start(f32[2,384,512]{2,0,1:T(2,128)} %copy.306) | copy-start | bytes 4718596
  248.3 7.5 %copy-start.35 = (f32[2,384,512]{2,0,1:T(2,128)S(1)}, f32[2,384,512]{2,0,1:T(2,128)}, u32[]{:S(2)}) copy-start(f32[2,384,512]{2,0,1:T(2,128)} %copy.307) | copy-start | bytes 4718596
  255.8 24.9 %copy-start = (f32[1,2,384,2048]{3,1,2,0:T(2,128)}, f32[1,2,384,2048]{3,1,2,0:T(2,128)S(1)}, u32[]{:S(2)}) copy-start(f32[1,2,384,2048]{3,1,2,0:T(2,128)S(1)} %maximum_bitcast_fusion) | copy-start | bytes 18874372
  259.6 21.2 %copy-start.1 = (f32[1,2,384,2048]{3,1,2,0:T(2,128)}, f32[1,2,384,2048]{3,1,2,0:T(2,128)S(1)}, u32[]{:S(2)}) copy-start(f32[1,2,384,2048]{3,1,2,0:T(2,128)S(1)} %maximum_bitcast_fusion.1) | copy-start | bytes 18874372
  279.0 256.7 %collective-permute-start.1 = (f32[2,2,128,2048]{3,1,2,0:T(2,128)}, f32[2,2,128,2048]{3,1,2,0:T(2,128)}, u32[]{:S(2)}, u32[]{:S(2)}) collective-permute-start(f32[2,2,128,2048]{3,1,2,0:T(2,128)} %slice.201), channel_id=1, source_target_pairs={{1,0},{2,1},{3,2},{4,3},{5,4},{6,5},{7,6},{8,7},{9,8},{10,9},{11,1... | collective-permute-start | bytes 12582920 | tf_op jit(solution)/shard_map/ppermute | solution.py:19
  433.6 5.2 copy-start.8
  433.6 5.2 copy-start.44
  433.6 5.2 copy-start.86
  436.3 4.5 copy-start.73
  436.3 4.7 copy-start.81
  436.3 4.9 copy-start.15
  436.3 4.9 copy-start.20
  454.4 81.2 %copy-start.90 = (f32[2]{0:T(128)S(1)}, f32[2]{0:T(128)}, u32[]{:S(2)}) copy-start(f32[2]{0:T(128)} %and_convert_fusion) | copy-start | bytes 28
  (66 other events, 140.7 us)
Sparse Core Ops, SparseCore 0:
  10.7 144.1 all-gather.9
  157.1 125.0 all-gather.7
  284.4 148.7 all-gather.11
  436.7 98.9 all-reduce.1
